TPU v7x, 128 devices: a whole 4x4x4 slice. The times are simulated.
128 devices in a mesh: row: 8 (over x_lo, z), col: 16 (over x_hi, y, core).
Axes of the slice: x: 4 (x_hi: 2, x_lo: 2; x = x_hi * 2 + x_lo), y: 4, z: 4, core: 2. Of those that a mesh axis runs over, the one named last changes fastest.
Arguments:
- features: bfloat16 [65536, 256], P(('col', 'row'))
- weight: bfloat16 [256, 256], replicated, may hold values from -0.375 to 0.375
- tiles: bfloat16 [8, 16, 384, 128, 128], P('row', 'col'), may hold values from -0.0546875 to 0.0546875
- tile_coords: int32 [8, 16, 2, 384], P('row', 'col'), may hold values from 0 to 63, as said below
- tile_counts: int32 [8, 16], P('row', 'col'), may hold values from 48 to 384, as said below
- cotangent: bfloat16 [65536, 256], P(('row', 'col')), may hold values from -6 to 6
Outputs:
- output: bfloat16 [65536, 256], P(('row', 'col'))
- feature_grad: bfloat16 [65536, 256], P(('col', 'row'))
- weight_grad: float32 [256, 256], replicated
Inputs may be any that keep to these rules, and one draw needn't show every extreme that they name: `tile_coords`: within one block the live and dead slots name distinct tiles; tile rows are below 64 and tile columns below 32. `tile_counts`: some block has all 384 slots live.
All inputs are finite; a program needn't handle non-finite values.
Results may differ from a plain program's by a relative error of at most 0.007.
Values may be sent and summed in bfloat16 or wider, within the bound.
A program may use at most 192 MiB of HBM per device.

v0:
```python
import jax
import jax.numpy as jnp
from jax import lax
from jax.sharding import PartitionSpec as P


def block_product(tile_block, tile_rows, tile_cols, live_count, panel_tiles, out_count, transpose):
    block = min(128, tile_block.shape[0])
    visit_bound = tile_block.shape[0] // block
    in_count = panel_tiles.shape[0]
    tile_side = panel_tiles.shape[1]
    channels = panel_tiles.shape[2]
    panel_flat = panel_tiles.reshape(in_count, tile_side * channels)

    def step(index, running):
        start = index * block
        values = lax.dynamic_slice_in_dim(tile_block, start, block, 0)
        rows_here = lax.dynamic_slice_in_dim(tile_rows, start, block, 0)
        cols_here = lax.dynamic_slice_in_dim(tile_cols, start, block, 0)
        slot_ids = start + jnp.arange(block, dtype=jnp.int32)
        live = (slot_ids < live_count).astype(jnp.float32)
        if transpose:
            source_ids = rows_here
            target = cols_here
        else:
            source_ids = cols_here
            target = rows_here
        pick = (source_ids[:, None] == jnp.arange(in_count, dtype=jnp.int32)[None, :]).astype(
            jnp.bfloat16
        )
        source = jnp.dot(pick, panel_flat, preferred_element_type=jnp.float32).astype(jnp.bfloat16)
        source = source.reshape(block, tile_side, channels)
        if transpose:
            product = jnp.einsum("tab,taf->tbf", values, source, preferred_element_type=jnp.float32)
        else:
            product = jnp.einsum("tab,tbf->taf", values, source, preferred_element_type=jnp.float32)
        placing = (jnp.arange(out_count, dtype=jnp.int32)[:, None] == target[None, :]).astype(
            jnp.float32
        )
        placing = placing * live[None, :]
        added = jnp.dot(
            placing,
            product.reshape(block, tile_side * channels),
            precision=lax.Precision.HIGHEST,
            preferred_element_type=jnp.float32,
        )
        return running + added

    start_value = jnp.zeros((out_count, tile_side * channels), jnp.float32)
    result = lax.fori_loop(0, visit_bound, step, start_value)
    return result.reshape(out_count, tile_side, channels)


def silu_parts(hidden, grad_in):
    sigma = jax.nn.sigmoid(hidden)
    output = (hidden * sigma).astype(jnp.bfloat16)
    hidden_grad = (grad_in.astype(jnp.float32) * sigma * (1.0 + hidden * (1.0 - sigma))).astype(
        jnp.bfloat16
    )
    return (output, hidden_grad)


def local(features, weight, tiles, tile_coords, tile_counts, cotangent):
    rows_total = lax.axis_size("row")
    cols_total = lax.axis_size("col")
    node_count = features.shape[0]
    channels = features.shape[1]
    tile_side = tiles.shape[-1]
    my_tiles = tiles[0, 0]
    tile_rows = tile_coords[0, 0, 0]
    tile_cols = tile_coords[0, 0, 1]
    live_count = tile_counts[0, 0]
    row_segments = cols_total * node_count // tile_side
    col_segments = rows_total * node_count // tile_side
    projected = jnp.dot(features, weight, preferred_element_type=jnp.float32).astype(jnp.bfloat16)
    col_panel = lax.all_gather(projected, "row", axis=0, tiled=True).reshape(
        col_segments, tile_side, channels
    )
    partial_value = block_product(
        my_tiles, tile_rows, tile_cols, live_count, col_panel, row_segments, False
    )
    partial_value = partial_value.reshape(row_segments * tile_side, channels)
    hidden = lax.psum_scatter(partial_value, "col", scatter_dimension=0, tiled=True)
    output, hidden_grad = silu_parts(hidden, cotangent)
    grad_panel = lax.all_gather(hidden_grad, "col", axis=0, tiled=True)
    grad_tiles = grad_panel.reshape(row_segments, tile_side, channels)
    back_partial = block_product(
        my_tiles, tile_rows, tile_cols, live_count, grad_tiles, col_segments, True
    )
    back_partial = back_partial.reshape(col_segments * tile_side, channels)
    projected_grad = lax.psum_scatter(back_partial, "row", scatter_dimension=0, tiled=True).astype(
        jnp.bfloat16
    )
    feature_grad = lax.dot_general(
        projected_grad, weight, (((1,), (1,)), ((), ())), preferred_element_type=jnp.float32
    ).astype(jnp.bfloat16)
    local_weight_grad = lax.dot_general(
        features, projected_grad, (((0,), (0,)), ((), ())), preferred_element_type=jnp.float32
    )
    weight_grad = lax.psum(local_weight_grad, ("row", "col"))
    return (output, feature_grad, weight_grad)


def solution(mesh):
    placed = (
        P(("col", "row"), None),
        P(),
        P("row", "col", None, None, None),
        P("row", "col", None, None),
        P("row", "col"),
        P(("row", "col"), None),
    )
    return jax.shard_map(
        local,
        mesh=mesh,
        in_specs=placed,
        out_specs=(P(("row", "col"), None), P(("col", "row"), None), P()),
        check_vma=False,
    )
```

profile of v0, /device:TPU:0, one launch (start us, length us, event | category | flops | bytes accessed | tf_op | source)
XLA Modules:
  0.0 813.6 jit_solution(6289081450679818959)
XLA Ops:
  10.8 43.8 %all-gather.3.cloned.1.call-done = bf16[4096,256]{1,0:T(8,128)(2,1)} async-done(((bf16[512,256]{1,0:T(8,128)(2,1)}), bf16[4096,256]{1,0:T(8,128)(2,1)}) %all-gather.3.cloned.1.call-update) | async-done | bytes 2097168 | tf_op jit(solution)/shard_map/all_gather | solution.py:76
  57.5 186.8 %while.28 = (s32[]{:T(128)}, f32[64,32768]{1,0:T(8,128)}, s32[384]{0:T(512)S(1)}, s32[]{:T(128)}, bf16[384,128,128]{2,1,0:T(8,128)(2,1)}, /*index=5*/s32[384]{0:...) while((s32[]{:T(128)}, f32[64,32768]{1,0:T(8,128)}, ...), condition=%wide.region_1.0_spmd.clone, body=%wide.region_0.0_spmd.clone.sunk | while | flops 4571812352 | bytes 123736240 | solution.py:50
  63.2 9.1 %copy.21 = bf16[16,8,128,256]{3,2,1,0:T(8,128)(2,1)} copy(bf16[16,8,128,256]{3,1,2,0:T(8,128)(2,1)} %bitcast.57) | data formatting | bytes 16777216 | tf_op jit(solution)/shard_map/while
  72.3 12.7 %fusion.47 = f32[128,128,256]{2,1,0:T(8,128)} fusion(bf16[128,128,256]{2,1,0:T(8,128)(2,1)} %bitcast.53, bf16[384,128,128]{2,1,0:T(8,128)(2,1)} %get-tuple-element.455, s32[]{:T(128)S(6)} %select_n.22), kind=kOutput, calls=%fused_computation.2.clone.1 | convolution fusion | flops 1073741824 | bytes 29360132 | tf_op jit(solution)/shard_map/while/body/eval_jaxpr/tab,tbf->taf/dot_general | solution.py:36
  85.0 17.7 %copy.22 = f32[16,8,128,256]{3,1,2,0:T(8,128)} copy(f32[16,8,128,256]{3,2,1,0:T(8,128)} %bitcast.51) | data formatting | bytes 33554432 | tf_op jit(solution)/shard_map/while
  103.4 15.6 %convolution_add_fusion.4 = f32[64,32768]{1,0:T(8,128)} fusion(f32[128,32768]{1,0:T(8,128)} %bitcast.56, f32[64,32768]{1,0:T(8,128)} %get-tuple-element.441, pred[]{:T(512)S(6)} %compare.6, f32[128]{0:T(128)S(1)} %compare_convert_fusion.4, s32[128]{0:T(128)S(1)} %dynamic_slice.60), kind=kOutput, calls=%fused_computation.1.clone.1 | convolution fusion | flops 3225436160 | bytes 33555456 | tf_op jit(solution)/shard_map/while/body/eval_jaxpr/dot_general | solution.py:41
  124.7 9.1 %copy.21 = bf16[16,8,128,256]{3,2,1,0:T(8,128)(2,1)} copy(bf16[16,8,128,256]{3,1,2,0:T(8,128)(2,1)} %bitcast.57) | data formatting | bytes 16777216 | tf_op jit(solution)/shard_map/while
  133.8 12.7 %fusion.47 = f32[128,128,256]{2,1,0:T(8,128)} fusion(bf16[128,128,256]{2,1,0:T(8,128)(2,1)} %bitcast.53, bf16[384,128,128]{2,1,0:T(8,128)(2,1)} %get-tuple-element.455, s32[]{:T(128)S(6)} %select_n.22), kind=kOutput, calls=%fused_computation.2.clone.1 | convolution fusion | flops 1073741824 | bytes 29360132 | tf_op jit(solution)/shard_map/while/body/eval_jaxpr/tab,tbf->taf/dot_general | solution.py:36
  146.5 17.7 %copy.22 = f32[16,8,128,256]{3,1,2,0:T(8,128)} copy(f32[16,8,128,256]{3,2,1,0:T(8,128)} %bitcast.51) | data formatting | bytes 33554432 | tf_op jit(solution)/shard_map/while
  164.9 16.8 %convolution_add_fusion.4 = f32[64,32768]{1,0:T(8,128)} fusion(f32[128,32768]{1,0:T(8,128)} %bitcast.56, f32[64,32768]{1,0:T(8,128)} %get-tuple-element.441, pred[]{:T(512)S(6)} %compare.6, f32[128]{0:T(128)S(1)} %compare_convert_fusion.4, s32[128]{0:T(128)S(1)} %dynamic_slice.60), kind=kOutput, calls=%fused_computation.1.clone.1 | convolution fusion | flops 3225436160 | bytes 33555456 | tf_op jit(solution)/shard_map/while/body/eval_jaxpr/dot_general | solution.py:41
  187.3 9.1 %copy.21 = bf16[16,8,128,256]{3,2,1,0:T(8,128)(2,1)} copy(bf16[16,8,128,256]{3,1,2,0:T(8,128)(2,1)} %bitcast.57) | data formatting | bytes 16777216 | tf_op jit(solution)/shard_map/while
  196.4 12.7 %fusion.47 = f32[128,128,256]{2,1,0:T(8,128)} fusion(bf16[128,128,256]{2,1,0:T(8,128)(2,1)} %bitcast.53, bf16[384,128,128]{2,1,0:T(8,128)(2,1)} %get-tuple-element.455, s32[]{:T(128)S(6)} %select_n.22), kind=kOutput, calls=%fused_computation.2.clone.1 | convolution fusion | flops 1073741824 | bytes 29360132 | tf_op jit(solution)/shard_map/while/body/eval_jaxpr/tab,tbf->taf/dot_general | solution.py:36
  209.2 17.7 %copy.22 = f32[16,8,128,256]{3,1,2,0:T(8,128)} copy(f32[16,8,128,256]{3,2,1,0:T(8,128)} %bitcast.51) | data formatting | bytes 33554432 | tf_op jit(solution)/shard_map/while
  227.6 16.8 %convolution_add_fusion.4 = f32[64,32768]{1,0:T(8,128)} fusion(f32[128,32768]{1,0:T(8,128)} %bitcast.56, f32[64,32768]{1,0:T(8,128)} %get-tuple-element.441, pred[]{:T(512)S(6)} %compare.6, f32[128]{0:T(128)S(1)} %compare_convert_fusion.4, s32[128]{0:T(128)S(1)} %dynamic_slice.60), kind=kOutput, calls=%fused_computation.1.clone.1 | convolution fusion | flops 3225436160 | bytes 33555456 | tf_op jit(solution)/shard_map/while/body/eval_jaxpr/dot_general | solution.py:41
  244.3 9.3 %reshape_reshape.13 = f32[8192,256]{1,0:T(8,128)} reshape(f32[64,32768]{1,0:T(8,128)} %get-tuple-element.251) | data formatting | bytes 16777216 | tf_op jit(solution)/shard_map/reshape;reshape | solution.py:82
  253.7 101.3 %reduce-scatter.3.cloned.1.call-done = f32[512,256]{1,0:T(8,128)} async-done(((f32[8192,256]{1,0:T(8,128)}), f32[512,256]{1,0:T(8,128)}) %reduce-scatter.3.cloned.1.call-update) | async-done | bytes 524304 | tf_op jit(solution)/shard_map/reduce_scatter | solution.py:83
  357.2 16.6 %copy.9 = bf16[1,1,384,128,128]{3,4,2,1,0:T(8,128)(2,1)} copy(bf16[1,1,384,128,128]{4,3,2,1,0:T(8,128)(2,1)} %bitcast.60) | data formatting | bytes 25165824 | tf_op args[2]
  373.8 38.3 %all-gather.5.cloned.1.call-done = bf16[8192,256]{1,0:T(8,128)(2,1)} async-done(((bf16[512,256]{1,0:T(8,128)(2,1)}), bf16[8192,256]{1,0:T(8,128)(2,1)}) %all-gather.5.cloned.1.call-update) | async-done | bytes 4194320 | tf_op jit(solution)/shard_map/all_gather | solution.py:85
  419.5 183.8 %while.29 = (s32[]{:T(128)}, f32[32,32768]{1,0:T(8,128)}, s32[384]{0:T(512)S(1)}, s32[]{:T(128)}, bf16[384,128,128]{1,2,0:T(8,128)(2,1)}, /*index=5*/s32[384]{0:...) while((s32[]{:T(128)}, f32[32,32768]{1,0:T(8,128)}, ...), condition=%wide.region_4.0_spmd.clone, body=%wide.region_3.0_spmd.clone.sunk | while | flops 3227533824 | bytes 117444784 | solution.py:50
  427.4 9.1 %copy.23 = bf16[16,8,128,256]{3,2,1,0:T(8,128)(2,1)} copy(bf16[16,8,128,256]{3,1,2,0:T(8,128)(2,1)} %bitcast.58) | data formatting | bytes 16777216 | tf_op jit(solution)/shard_map/while
  436.5 12.7 %fusion.53 = f32[128,128,256]{2,1,0:T(8,128)} fusion(bf16[128,128,256]{2,1,0:T(8,128)(2,1)} %bitcast.54, bf16[384,128,128]{1,2,0:T(8,128)(2,1)} %get-tuple-element.488, s32[]{:T(128)S(6)} %select_n.23), kind=kOutput, calls=%fused_computation.16.clone.1 | convolution fusion | flops 1073741824 | bytes 29360132 | tf_op jit(solution)/shard_map/while/body/eval_jaxpr/tab,taf->tbf/dot_general | solution.py:34
  449.2 17.7 %copy.24 = f32[16,8,128,256]{3,1,2,0:T(8,128)} copy(f32[16,8,128,256]{3,2,1,0:T(8,128)} %bitcast.52) | data formatting | bytes 33554432 | tf_op jit(solution)/shard_map/while
  467.6 12.6 %convolution_add_fusion.5 = f32[32,32768]{1,0:T(8,128)} fusion(f32[128,32768]{1,0:T(8,128)} %bitcast.55, f32[32,32768]{1,0:T(8,128)} %get-tuple-element.474, pred[]{:T(512)S(6)} %compare.7, f32[128]{0:T(128)S(1)} %compare_convert_fusion.5, s32[128]{0:T(128)S(1)} %dynamic_slice.63), kind=kOutput, calls=%fused_computation.15.clone.1 | convolution fusion | flops 1612718080 | bytes 25166848 | tf_op jit(solution)/shard_map/while/body/eval_jaxpr/dot_general | solution.py:41
  488.1 9.1 %copy.23 = bf16[16,8,128,256]{3,2,1,0:T(8,128)(2,1)} copy(bf16[16,8,128,256]{3,1,2,0:T(8,128)(2,1)} %bitcast.58) | data formatting | bytes 16777216 | tf_op jit(solution)/shard_map/while
  497.2 12.7 %fusion.53 = f32[128,128,256]{2,1,0:T(8,128)} fusion(bf16[128,128,256]{2,1,0:T(8,128)(2,1)} %bitcast.54, bf16[384,128,128]{1,2,0:T(8,128)(2,1)} %get-tuple-element.488, s32[]{:T(128)S(6)} %select_n.23), kind=kOutput, calls=%fused_computation.16.clone.1 | convolution fusion | flops 1073741824 | bytes 29360132 | tf_op jit(solution)/shard_map/while/body/eval_jaxpr/tab,taf->tbf/dot_general | solution.py:34
  509.9 17.7 %copy.24 = f32[16,8,128,256]{3,1,2,0:T(8,128)} copy(f32[16,8,128,256]{3,2,1,0:T(8,128)} %bitcast.52) | data formatting | bytes 33554432 | tf_op jit(solution)/shard_map/while
  528.3 13.4 %convolution_add_fusion.5 = f32[32,32768]{1,0:T(8,128)} fusion(f32[128,32768]{1,0:T(8,128)} %bitcast.55, f32[32,32768]{1,0:T(8,128)} %get-tuple-element.474, pred[]{:T(512)S(6)} %compare.7, f32[128]{0:T(128)S(1)} %compare_convert_fusion.5, s32[128]{0:T(128)S(1)} %dynamic_slice.63), kind=kOutput, calls=%fused_computation.15.clone.1 | convolution fusion | flops 1612718080 | bytes 25166848 | tf_op jit(solution)/shard_map/while/body/eval_jaxpr/dot_general | solution.py:41
  558.8 12.7 %fusion.53 = f32[128,128,256]{2,1,0:T(8,128)} fusion(bf16[128,128,256]{2,1,0:T(8,128)(2,1)} %bitcast.54, bf16[384,128,128]{1,2,0:T(8,128)(2,1)} %get-tuple-element.488, s32[]{:T(128)S(6)} %select_n.23), kind=kOutput, calls=%fused_computation.16.clone.1 | convolution fusion | flops 1073741824 | bytes 29360132 | tf_op jit(solution)/shard_map/while/body/eval_jaxpr/tab,taf->tbf/dot_general | solution.py:34
  571.5 17.7 %copy.24 = f32[16,8,128,256]{3,1,2,0:T(8,128)} copy(f32[16,8,128,256]{3,2,1,0:T(8,128)} %bitcast.52) | data formatting | bytes 33554432 | tf_op jit(solution)/shard_map/while
  589.9 13.4 %convolution_add_fusion.5 = f32[32,32768]{1,0:T(8,128)} fusion(f32[128,32768]{1,0:T(8,128)} %bitcast.55, f32[32,32768]{1,0:T(8,128)} %get-tuple-element.474, pred[]{:T(512)S(6)} %compare.7, f32[128]{0:T(128)S(1)} %compare_convert_fusion.5, s32[128]{0:T(128)S(1)} %dynamic_slice.63), kind=kOutput, calls=%fused_computation.15.clone.1 | convolution fusion | flops 1612718080 | bytes 25166848 | tf_op jit(solution)/shard_map/while/body/eval_jaxpr/dot_general | solution.py:41
  608.3 51.3 %reduce-scatter.5.cloned.1.call-done = f32[512,256]{1,0:T(8,128)} async-done(((f32[4096,256]{1,0:T(8,128)}), f32[512,256]{1,0:T(8,128)}) %reduce-scatter.5.cloned.1.call-update) | async-done | bytes 524304 | tf_op jit(solution)/shard_map/reduce_scatter | solution.py:91
  663.6 141.7 %all-reduce.2.cloned.1.call-done = f32[256,256]{0,1:T(8,128)} async-done(((f32[256,256]{0,1:T(8,128)}), f32[256,256]{0,1:T(8,128)}) %all-reduce.2.cloned.1.call-update) | async-done | bytes 262160 | tf_op jit(solution)/shard_map/psum | solution.py:100
  (52 shorter events, 80.9 us)
Async XLA Ops:
  7.2 1.0 copy-start
  7.2 47.4 %all-gather.3.cloned.1.call-start = ((), (), s32[]{:S(2)}) async-start(), calls=%async_computation.2 | async-start | bytes 2359296 | tf_op jit(solution)/shard_map/all_gather | solution.py:76
  10.0 345.1 %reduce-scatter.3.cloned.1.call-start = ((), (), s32[]{:S(2)}) async-start(), calls=%async_computation.3 | async-start | bytes 8912896 | tf_op jit(solution)/shard_map/reduce_scatter | solution.py:83
  253.6 101.4 %copy-start.2 = (bf16[512,256]{1,0:T(8,128)(2,1)S(1)}, bf16[512,256]{1,0:T(8,128)(2,1)}, u32[]{:S(2)}) copy-start(bf16[512,256]{1,0:T(8,128)(2,1)} %param.15) | copy-start | bytes 786436
  253.6 158.5 %all-gather.5.cloned.1.call-start = ((), (), s32[]{:S(2)}) async-start(), calls=%async_computation.4 | async-start | bytes 4456448 | tf_op jit(solution)/shard_map/all_gather | solution.py:85
  357.1 302.4 %reduce-scatter.5.cloned.1.call-start = ((), (), s32[]{:S(2)}) async-start(), calls=%async_computation.5 | async-start | bytes 4718592 | tf_op jit(solution)/shard_map/reduce_scatter | solution.py:91
  603.3 58.3 %copy-start.1 = (bf16[256,256]{1,0:T(8,128)(2,1)S(1)}, bf16[256,256]{1,0:T(8,128)(2,1)}, u32[]{:S(2)}) copy-start(bf16[256,256]{1,0:T(8,128)(2,1)} %param.11) | copy-start | bytes 393220
  608.3 197.1 %all-reduce.2.cloned.1.call-start = ((), (), s32[]{:S(2)}) async-start(), calls=%async_computation.6 | async-start | bytes 524288 | tf_op jit(solution)/shard_map/psum | solution.py:100
Sparse Core Ops, SparseCore 0:
  10.2 44.3 all-gather.2
  253.8 101.2 reduce-scatter.2
  358.1 53.9 all-gather.4
  608.4 51.1 reduce-scatter.4
  664.8 140.5 all-reduce.1
where the time goes:
time: 816 us; the launch traced here: 814 us
  waiting for transfers between devices  376 us (46%)
  matrix products  211 us (26%)
  local copies, waits for them, and re-layouts  206 us (25%)
  between operations  13.8 us (2%)
    while x12, local copies, waits for them, and re-layouts  161 us
    psum x1, waiting for transfers between devices, local(): weight_grad = lax.psum(local_weight_grad, ('row', 'col'))  142 us
    reduce_scatter x1, waiting for transfers between devices, local(): lax.psum_scatter(partial_value, 'col', scatter_dimension=0, tiled=True)  101 us
    dot_general x6, matrix products, step(): jnp.dot(placing, product.reshape(block, tile_side * channels), precision=...  88.6 us
    reduce_scatter x1, waiting for transfers between devices, local(): lax.psum_scatter(back_partial, 'row', scatter_dimension=0, tiled=True)  51.3 us
    all_gather x1, waiting for transfers between devices, local(): lax.all_gather(projected, 'row', axis=0, tiled=True)  43.8 us
    dot_general x6, matrix products, step(): jnp.dot(pick, panel_flat, preferred_element_type=jnp.float32)  40.2 us
    all_gather x1, waiting for transfers between devices, local(): grad_panel = lax.all_gather(hidden_grad, 'col', axis=0, tiled=True)  38.3 us
  transfers between devices with their start and end apart: 5, of which 5 were waited for; matrix products, arithmetic and copies ran while one was open for 2% of the time, Pallas kernels for 0%

commit v1 on v0

v1 whole, which is shorter than its diff:
```python
import functools

import jax
import jax.numpy as jnp
from jax import lax
from jax.experimental import pallas as pl
from jax.experimental.pallas import tpu as pltpu
from jax.sharding import PartitionSpec as P

MESH = pl.DeviceIdType.MESH
BF = jnp.bfloat16
F32 = jnp.float32
ANY = pl.BlockSpec(memory_space=pl.ANY)
VMEM = pl.BlockSpec(memory_space=pltpu.VMEM)
SMEM = pl.BlockSpec(memory_space=pltpu.SMEM)
VMEM_BYTES = 60 * 2**20
SIDE = 128
FEAT = 256
SLOTS = 384
CHUNK = 32
H = (pl.ds(0, 2), pl.ds(2, 2))


class Group:
    def __init__(self, along):
        row = lax.axis_index("row")
        col = lax.axis_index("col")
        if along == "row":
            place = row
            self.device = lambda g: (g, col)
        else:
            place = lax.div(col, 2)
            core = lax.rem(col, 2)
            self.device = lambda g: (row, g * 2 + core)
            self.sibling = (row, place * 2 + 1 - core)
            self.core = core
        a = lax.div(place, 4)
        b = lax.rem(place, 4)
        up = lax.rem(b + 1, 4)
        down = lax.rem(b + 3, 4)
        far = lax.rem(b + 2, 4)
        self.own = place
        self.up, self.down, self.far = a * 4 + up, a * 4 + down, a * 4 + far
        self.other = (1 - a) * 4 + b
        self.other_up, self.other_down, self.other_far = (
            (1 - a) * 4 + up,
            (1 - a) * 4 + down,
            (1 - a) * 4 + far,
        )

    def peers(self):
        return [self.device(g) for g in (self.up, self.down, self.far, self.other)]


def greet(peers):
    barrier = pltpu.get_barrier_semaphore()
    for peer in peers:
        pl.semaphore_signal(barrier, inc=1, device_id=peer, device_id_type=MESH)
    pl.semaphore_wait(barrier, len(peers))


def ring_sum(group, send, whole, size, got, met, out, base):
    rows = lambda b: pl.ds(b * size, size)
    ring = [(group.device(g), lax.rem(g, 4)) for g in (group.up, group.down, group.far)]
    mine = lax.rem(group.own, 4)
    copies = [send(whole.at[rows(b)], got.at[k], peer) for k, (peer, b) in enumerate(ring)]
    yield
    for copy in copies:
        copy.wait_recv()
    met[0] = whole[rows(mine)] + got[0] + got[1] + got[2]
    copy = send(met.at[0], met.at[1], group.device(group.other))
    yield
    copy.wait_recv()
    spot = out.at[pl.ds(base + mine * size, size)]
    spot[...] = met[0] + met[1]
    copies = [send(spot, spot, peer) for peer, _ in ring]
    yield
    for copy in copies:
        copy.wait_recv()


def pair_then_ring_sum(group, send, whole, theirs, half, got, met, out):
    size = whole.shape[0] // 2
    mine = pl.ds(group.core * size, size)
    copy = send(whole.at[pl.ds((1 - group.core) * size, size)], theirs, group.sibling)
    yield
    copy.wait_recv()
    half[...] = whole[mine] + theirs[...]
    yield from ring_sum(group, send, half, size // 4, got, met, out, group.core * size)
    copy = send(out.at[mine], out.at[mine], group.sibling)
    yield
    copy.wait_recv()


class Sender:
    def __init__(self, send_sem, recv_sem):
        self.send_sem, self.recv_sem = send_sem, recv_sem
        self.used = 0
        self.all = []

    def __call__(self, src, dst, device):
        copy = pltpu.make_async_remote_copy(
            src_ref=src,
            dst_ref=dst,
            send_sem=self.send_sem.at[self.used],
            recv_sem=self.recv_sem.at[self.used],
            device_id=device,
            device_id_type=MESH,
        )
        self.used += 1
        self.all.append(copy)
        copy.start()
        return copy

    def finish(self):
        for copy in self.all:
            copy.wait_send()


def gather(group, send, own, spot, landed, tick=lambda: None):
    up, down, other = (group.device(g) for g in (group.up, group.down, group.other))
    here = spot(group.own)
    c_up, c_down, c_other = [None, None], [None, None], [None, None]
    for h in (0, 1):
        c_up[h] = send(own.at[H[h]], here.at[H[h]], up)
        c_down[1 - h] = send(own.at[H[1 - h]], here.at[H[1 - h]], down)
        c_other[h] = send(own.at[H[h]], here.at[H[h]], other)
    tick()
    f_up, f_down = [None, None], [None, None]
    c_up[0].wait_recv()
    far_first = send(spot(group.down).at[H[0]], spot(group.down).at[H[0]], up)
    landed(group.down, 0)
    c_down[1].wait_recv()
    far_second = send(spot(group.up).at[H[1]], spot(group.up).at[H[1]], down)
    landed(group.up, 1)
    for h in (0, 1):
        c_other[h].wait_recv()
        block = spot(group.other).at[H[h]]
        f_up[h] = send(block, block, up)
        f_down[h] = send(block, block, down)
        landed(group.other, h)
    tick()
    c_up[1].wait_recv()
    landed(group.down, 1)
    c_down[0].wait_recv()
    landed(group.up, 0)
    far_first.wait_recv()
    block = spot(group.far).at[H[0]]
    x_first = send(block, block, other)
    landed(group.far, 0)
    far_second.wait_recv()
    block = spot(group.far).at[H[1]]
    x_second = send(block, block, other)
    landed(group.far, 1)
    tick()
    for h in (0, 1):
        f_up[h].wait_recv()
        landed(group.other_down, h)
        f_down[h].wait_recv()
        landed(group.other_up, h)
    x_first.wait_recv()
    landed(group.other_far, 0)
    x_second.wait_recv()
    landed(group.other_far, 1)


def plus(target, *terms):
    total = terms[0][...].astype(F32)
    for term in terms[1:]:
        total = total + term[...].astype(F32)
    target[...] = total.astype(target.dtype)


def scatter_sum(group, send, ready, spot, got, tick=lambda: None):
    r1, r2d, r2u, r3, r4d, r4u, r5 = (got.at[k] for k in range(7))
    up, down, other = (group.device(g) for g in (group.up, group.down, group.other))
    ready(group.other_far)
    c1 = [send(spot(group.other_far).at[H[h]], r1.at[H[h]], other) for h in (0, 1)]
    ready(group.other_up)
    c2u = [send(spot(group.other_up).at[H[h]], r2d.at[H[h]], up) for h in (0, 1)]
    ready(group.other_down)
    c2d = [send(spot(group.other_down).at[H[h]], r2u.at[H[h]], down) for h in (0, 1)]
    ready(group.up)
    c4u, c4d = [None, None], [None, None]
    c4u[1] = send(spot(group.up).at[H[1]], r4d.at[H[1]], up)
    ready(group.down)
    c4d[0] = send(spot(group.down).at[H[0]], r4u.at[H[0]], down)
    ready(group.far)
    tick()
    c1[0].wait_recv()
    plus(r1.at[H[0]], r1.at[H[0]], spot(group.far).at[H[0]])
    c3u = send(r1.at[H[0]], r3.at[H[0]], up)
    tick()
    c1[1].wait_recv()
    plus(r1.at[H[1]], r1.at[H[1]], spot(group.far).at[H[1]])
    c3d = send(r1.at[H[1]], r3.at[H[1]], down)
    ready(group.other)
    tick()
    c5 = []
    for h in (0, 1):
        c2u[h].wait_recv()
        c2d[h].wait_recv()
        plus(r2d.at[H[h]], r2d.at[H[h]], r2u.at[H[h]], spot(group.other).at[H[h]])
        c5.append(send(r2d.at[H[h]], r5.at[H[h]], other))
        tick()
    c3u.wait_recv()
    plus(r3.at[H[0]], r3.at[H[0]], spot(group.up).at[H[0]])
    c4u[0] = send(r3.at[H[0]], r4d.at[H[0]], up)
    c3d.wait_recv()
    plus(r3.at[H[1]], r3.at[H[1]], spot(group.down).at[H[1]])
    c4d[1] = send(r3.at[H[1]], r4u.at[H[1]], down)
    ready(group.own)
    for copies in (c5, c4u, c4d):
        for copy in copies:
            copy.wait_recv()
    return (spot(group.own), r4d, r4u, r5)


def gather_features(own_ref, out_ref, send_sem, recv_sem, local_sem):
    group = Group("row")
    greet([group.device(g) for g in (group.up, group.down, group.other)])
    send = Sender(send_sem, recv_sem)
    mine = pltpu.make_async_copy(own_ref, out_ref.at[group.own], local_sem)
    mine.start()
    gather(group, send, own_ref, lambda g: out_ref.at[g], lambda g, h: None)
    mine.wait()
    send.finish()


def tile_sums(transpose, coords, count_ref, panel_hbm, tiles_hbm, out_hbm, tiles, panel, acc, out, sems):
    count = count_ref[0, 0]
    panel_copy = pltpu.make_async_copy(panel_hbm, panel, sems.at[0])
    panel_copy.start()
    chunks = SLOTS // CHUNK

    def fetch(k):
        part = pl.ds(k * CHUNK, CHUNK)
        return pltpu.make_async_copy(tiles_hbm.at[part], tiles.at[part], sems.at[k + 1])

    def begin(k, _):
        @pl.when(k * CHUNK < count)
        def _():
            fetch(k).start()

        return 0

    lax.fori_loop(0, chunks, begin, 0)
    outs = out.shape[0]

    def clear(k, _):
        acc[k] = jnp.zeros(acc.shape[1:], F32)
        return 0

    lax.fori_loop(0, outs, clear, 0)
    panel_copy.wait()
    unroll = 8

    def step(s):
        row, column = coords[0, s], coords[1, s]
        source, target = (row, column) if transpose else (column, row)
        target = jnp.where(s < count, target, outs)
        if transpose:
            product = jnp.dot(panel[source], tiles[s], preferred_element_type=F32)
        else:
            product = jnp.dot(tiles[s], panel[source], preferred_element_type=F32)
        acc[target] += product

    def chunk(k, _):
        @pl.when(k * CHUNK < count)
        def _():
            fetch(k).wait()

            def several(i, _):
                for u in range(unroll):
                    step(k * CHUNK + i * unroll + u)
                return 0

            left = jnp.minimum(count - k * CHUNK, CHUNK)
            lax.fori_loop(0, lax.div(left + unroll - 1, unroll), several, 0)

        return 0

    lax.fori_loop(0, chunks, chunk, 0)
    parts = 4
    size = outs // parts
    copies = []
    for p in range(parts):

        def narrow(k, _):
            out[k] = acc[k].astype(BF)
            return 0

        lax.fori_loop(p * size, (p + 1) * size, narrow, 0)
        part = pl.ds(p * size, size)
        copy = pltpu.make_async_copy(out.at[part], out_hbm.at[part], sems.at[chunks + 1 + p])
        copy.start()
        copies.append(copy)
    for copy in copies:
        copy.wait()


def middle(
    part_hbm, weight, cotangent, output, grads, weight_grad,
    part, theirs, got, total_hi, total_lo, own, whole, ring_got, ring_met, send_sem, recv_sem, local_sem,
):
    group = Group("col")
    rows_group = Group("row")
    core = group.core
    load = pltpu.make_async_copy(part_hbm, part, local_sem)
    load.start()
    greet([group.device(g) for g in (group.up, group.down, group.other)] + [group.sibling] + rows_group.peers())
    send = Sender(send_sem, recv_sem)
    order = (
        group.other_far, group.other_up, group.other_down, group.up,
        group.down, group.far, group.other, group.own,
    )
    pairs = []
    for k, g in enumerate(order):
        source = part_hbm.at[pl.ds((g * 2 + 1 - core) * 4, 4)]
        pairs.append(send(source, theirs.at[k], group.sibling))
    load.wait()
    step = iter(range(len(order)))
    held = {}

    def ready(g):
        k = next(step)
        pairs[k].wait_recv()
        held[id(g)] = k
        mine = part.at[pl.ds((g * 2 + core) * 4, 4)]
        for h in (0, 1):
            plus(theirs.at[k, H[h]], theirs.at[k, H[h]], mine.at[H[h]])

    terms = scatter_sum(group, send, ready, lambda g: theirs.at[held[id(g)]], got)
    for t in range(4):
        total = terms[0][t].astype(F32)
        for term in terms[1:]:
            total = total + term[t].astype(F32)
        rows = pl.ds(t * SIDE, SIDE)
        high = total.astype(BF)
        low = (total - high.astype(F32)).astype(BF)
        total_hi[rows] = high
        total_lo[rows] = low
        hidden = jnp.dot(high, weight[...], preferred_element_type=F32) + jnp.dot(
            low, weight[...], preferred_element_type=F32
        )
        sigma = 1.0 / (1.0 + jnp.exp(-hidden))
        output[rows] = (hidden * sigma).astype(BF)
        slope = (cotangent[rows].astype(F32) * sigma * (1.0 + hidden * (1.0 - sigma))).astype(BF)
        own[rows] = slope
        grads[group.own * 8 + core * 4 + t] = lax.dot_general(
            weight[...], slope, (((1,), (1,)), ((), ())), preferred_element_type=F32
        ).astype(BF)

    def spot(g):
        return grads.at[pl.ds((g * 2 + core) * 4, 4)]

    def landed(g, h):
        block = spot(g).at[H[h]]
        back.append(send(block, block, group.sibling))

    back = []
    landed(group.own, 0)
    landed(group.own, 1)

    def weight_sum():
        over = (((0,), (0,)), ((), ()))
        whole[...] = lax.dot_general(
            total_hi[...], own[...], over, preferred_element_type=F32
        ) + lax.dot_general(total_lo[...], own[...], over, preferred_element_type=F32)
        yield from ring_sum(rows_group, send, whole, FEAT // 4, ring_got, ring_met, weight_grad, 0)

    stages = weight_sum()
    gather(group, send, spot(group.own), spot, landed, lambda: next(stages, None))
    for _ in stages:
        pass
    for copy in back:
        copy.wait_recv()
    send.finish()


def last_sum(part, weight_part, out, weight_grad, got, theirs, half, ring_got, ring_met, send_sem, recv_sem):
    group = Group("row")
    cols_group = Group("col")
    greet([group.device(g) for g in (group.up, group.down, group.other)] + [cols_group.sibling] + cols_group.peers())
    send = Sender(send_sem, recv_sem)
    stages = pair_then_ring_sum(cols_group, send, weight_part, theirs, half, ring_got, ring_met, weight_grad)
    terms = scatter_sum(
        group, send, lambda g: None, lambda g: part.at[pl.ds(g * 4, 4)], got, lambda: next(stages, None)
    )
    for _ in stages:
        pass
    for t in range(4):
        total = terms[0][t].astype(F32)
        for term in terms[1:]:
            total = total + term[t].astype(F32)
        out[pl.ds(t * SIDE, SIDE)] = total.T.astype(BF)
    send.finish()


def params(collective_id=None):
    if collective_id is None:
        return pltpu.CompilerParams(vmem_limit_bytes=VMEM_BYTES)
    return pltpu.CompilerParams(
        collective_id=collective_id, has_side_effects=True, vmem_limit_bytes=VMEM_BYTES
    )


def sems(n):
    return [pltpu.SemaphoreType.DMA((n,)), pltpu.SemaphoreType.DMA((n,))]


def run_tiles(transpose, coords, count, panel, tiles):
    outs = 32 if transpose else 64
    ins = 64 if transpose else 32
    block = (FEAT, SIDE) if transpose else (SIDE, FEAT)
    return pl.pallas_call(
        functools.partial(tile_sums, transpose),
        out_shape=jax.ShapeDtypeStruct((outs,) + block, BF),
        in_specs=[SMEM, SMEM, ANY, ANY],
        out_specs=ANY,
        scratch_shapes=[
            pltpu.VMEM((SLOTS, SIDE, SIDE), BF),
            pltpu.VMEM((ins,) + block, BF),
            pltpu.VMEM((outs + 1,) + block, F32),
            pltpu.VMEM((outs,) + block, BF),
            pltpu.SemaphoreType.DMA((SLOTS // CHUNK + 5,)),
        ],
        compiler_params=params(),
        name="tiles_back" if transpose else "tiles_forward",
    )(coords, count, panel, tiles)


def run_gather(features):
    return pl.pallas_call(
        gather_features,
        out_shape=jax.ShapeDtypeStruct((8, 4, SIDE, FEAT), BF),
        in_specs=[VMEM],
        out_specs=VMEM,
        scratch_shapes=sems(14) + [pltpu.SemaphoreType.DMA],
        compiler_params=params(0),
        name="gather_features",
    )(features.reshape(4, SIDE, FEAT))


def run_middle(part, weight, cotangent):
    nodes = 4 * SIDE
    return pl.pallas_call(
        middle,
        out_shape=(
            jax.ShapeDtypeStruct((nodes, FEAT), BF),
            jax.ShapeDtypeStruct((64, FEAT, SIDE), BF),
            jax.ShapeDtypeStruct((FEAT, FEAT), F32),
        ),
        in_specs=[ANY, VMEM, VMEM],
        out_specs=(VMEM, VMEM, VMEM),
        scratch_shapes=[
            pltpu.VMEM((64, SIDE, FEAT), BF),
            pltpu.VMEM((8, 4, SIDE, FEAT), BF),
            pltpu.VMEM((7, 4, SIDE, FEAT), BF),
            pltpu.VMEM((nodes, FEAT), BF),
            pltpu.VMEM((nodes, FEAT), BF),
            pltpu.VMEM((nodes, FEAT), BF),
            pltpu.VMEM((FEAT, FEAT), F32),
            pltpu.VMEM((3, FEAT // 4, FEAT), F32),
            pltpu.VMEM((2, FEAT // 4, FEAT), F32),
        ]
        + sems(59)
        + [pltpu.SemaphoreType.DMA],
        compiler_params=params(1),
        name="middle",
    )(part, weight, cotangent)


def run_last(part, weight_part):
    return pl.pallas_call(
        last_sum,
        out_shape=(
            jax.ShapeDtypeStruct((4 * SIDE, FEAT), BF),
            jax.ShapeDtypeStruct((FEAT, FEAT), F32),
        ),
        in_specs=[VMEM, VMEM],
        out_specs=(VMEM, VMEM),
        scratch_shapes=[
            pltpu.VMEM((7, 4, FEAT, SIDE), BF),
            pltpu.VMEM((FEAT // 2, FEAT), F32),
            pltpu.VMEM((FEAT // 2, FEAT), F32),
            pltpu.VMEM((3, FEAT // 8, FEAT), F32),
            pltpu.VMEM((2, FEAT // 8, FEAT), F32),
        ]
        + sems(23),
        compiler_params=params(2),
        name="last_sum",
    )(part, weight_part)


def local(features, weight, tiles, tile_coords, tile_counts, cotangent):
    my_tiles, coords = tiles[0, 0], tile_coords[0, 0]
    panel = run_gather(features).reshape(32, SIDE, FEAT)
    part = run_tiles(False, coords, tile_counts, panel, my_tiles)
    output, grads, local_weight_grad = run_middle(part, weight, cotangent)
    back = run_tiles(True, coords, tile_counts, grads, my_tiles)
    feature_grad, weight_grad = run_last(back, local_weight_grad)
    return (output, feature_grad, weight_grad)


def solution(mesh):
    placed = (
        P(("col", "row"), None),
        P(),
        P("row", "col", None, None, None),
        P("row", "col", None, None),
        P("row", "col"),
        P(("row", "col"), None),
    )
    return jax.shard_map(
        local,
        mesh=mesh,
        in_specs=placed,
        out_specs=(P(("row", "col"), None), P(("col", "row"), None), P()),
        check_vma=False,
    )
```

time: 816 us -> 138 us (0.17)
  waiting for transfers between devices: 376 us -> 0 us
  matrix products: 211 us -> 0 us
  local copies, waits for them, and re-layouts: 206 us -> 4.05 us
  Pallas kernels: 0 us -> 132 us
  between operations: 13.8 us -> 1.33 us
    dot_general x21 -> x0, matrix products: 211 us -> none  [the longest x6 88.6 us: step(): jnp.dot(placing, product.reshape(block, tile_side * channels), precision=...]
    while x12 -> x0, local copies, waits for them, and re-layouts: 161 us -> none
    reduce_scatter x2 -> x0, waiting for transfers between devices: 153 us -> none  [the longest x1 101 us: local(): lax.psum_scatter(partial_value, 'col', scatter_dimension=0, tiled=True)]
    psum x1 -> x0, waiting for transfers between devices: 142 us -> none  [local(): weight_grad = lax.psum(local_weight_grad, ('row', 'col'))]
    pallas_call x0 -> x5, Pallas kernels: none -> 132 us  [the longest x1 53.9 us: run_middle(): pl.pallas_call(middle, out_shape=(jax.ShapeDtypeStruct((nodes, FEAT), BF)...]
    all_gather x2 -> x0, waiting for transfers between devices: 82.1 us -> none  [the longest x1 43.8 us: local(): lax.all_gather(projected, 'row', axis=0, tiled=True)]
    another operation x4 -> x0, local copies, waits for them, and re-layouts: 24.5 us -> none  [the longest x2 10.3 us: block_product(): panel_flat = panel_tiles.reshape(in_count, tile_side * channels)]
    unnamed x8 -> x5, local copies, waits for them, and re-layouts: 19.3 us -> 4.05 us
  transfers between devices with their start and end apart: 5 -> 0, of which waited for: 5 -> 0; matrix products, arithmetic and copies ran while one was open for 2% -> 0% of each run, Pallas kernels for 0% -> 0%
where the time goes in v1:
time: 138 us
  Pallas kernels  132 us (96%)
  local copies, waits for them, and re-layouts  4.05 us (3%)
    pallas_call x1, Pallas kernels, run_middle(): pl.pallas_call(middle, out_shape=(jax.ShapeDtypeStruct((nodes, FEAT), BF)...  53.9 us
    pallas_call x1, Pallas kernels, run_last(): pl.pallas_call(last_sum, out_shape=(jax.ShapeDtypeStruct((4 * SIDE, FEAT)...  35.3 us
    pallas_call x1, Pallas kernels, run_gather(): pl.pallas_call(gather_features, out_shape=jax.ShapeDtypeStruct((8, 4, SID...  23.4 us
    pallas_call x2, Pallas kernels, run_tiles(): pl.pallas_call(functools.partial(tile_sums, transpose), out_shape=jax.Sha...  19.6 us
    unnamed x5, local copies, waits for them, and re-layouts  4.05 us

profile of v1, /device:TPU:0, one launch (start us, length us, event | category | flops | bytes accessed | tf_op | source)
XLA Modules:
  0.0 137.6 jit_solution(12562381649368631376)
XLA Ops:
  1.3 23.4 %gather_features.1 = bf16[8,4,128,256]{3,2,1,0:T(8,128)(2,1)} custom-call(bf16[4,128,256]{2,1,0:T(8,128)(2,1)} %bitcast.7), custom_call_target="tpu_custom_call" | custom-call | tf_op jit(solution)/shard_map/gather_features/pallas_call | solution.py:434
  24.7 9.8 %tiles_forward.1.part_hbm = bf16[64,128,256]{2,1,0:T(8,128)(2,1)} custom-call(s32[2,384]{1,0:T(2,128)} %bitcast.8, s32[1,1]{1,0:T(1,128)S(6)} %copy.12.count_ref, bf16[32,128,256]{2,1,0:T(8,128)(2,1)} %bitcast.6, bf16[384,128,128]{2,1,0:T(8,128)(2,1)} %bitcast.4), custom_call_target="tpu_custom_call" | custom-call | tf_op jit(solution)/shard_map/tiles_forward/pallas_call | solution.py:416
  34.5 53.9 %middle.1 = (bf16[512,256]{1,0:T(8,128)(2,1)}, bf16[64,256,128]{2,1,0:T(8,128)(2,1)}, f32[256,256]{1,0:T(8,128)}) custom-call(bf16[64,128,256]{2,1,0:T(8,128)(2,1)} %tiles_forward.1.part_hbm, bf16[256,256]{1,0:T(8,128)(2,1)} %weight.1, bf16[512,256]{1,0:T(8,128)(2,1)} %cotangent.1), custom_call_target="tpu_custom_call" | custom-call | tf_op jit(solution)/shard_map/middle/pallas_call | solution.py:447
  88.4 0.0 copy-start
  88.4 9.8 %tiles_back.1.part = bf16[32,256,128]{2,1,0:T(8,128)(2,1)} custom-call(s32[2,384]{1,0:T(2,128)} %bitcast.9, s32[1,1]{1,0:T(1,128)S(6)} %copy.12.count_ref, bf16[64,256,128]{2,1,0:T(8,128)(2,1)} %get-tuple-element.9.panel_hbm, bf16[384,128,128]{2,1,0:T(8,128)(2,1)} %bitcast.5), custom_call_target="tpu_custom_call" | custom-call | tf_op jit(solution)/shard_map/tiles_back/pallas_call | solution.py:416
  98.2 35.3 %last_sum.1 = (bf16[512,256]{1,0:T(8,128)(2,1)}, f32[256,256]{1,0:T(8,128)}) custom-call(bf16[32,256,128]{2,1,0:T(8,128)(2,1)} %tiles_back.1.part, f32[256,256]{1,0:T(8,128)} %get-tuple-element.10.weight_part), custom_call_target="tpu_custom_call" | custom-call | tf_op jit(solution)/shard_map/last_sum/pallas_call | solution.py:475
  133.5 0.0 copy-done
  133.5 0.7 copy.13
  134.2 1.7 %copy.14 = bf16[512,256]{1,0:T(8,128)(2,1)} copy(bf16[512,256]{1,0:T(8,128)(2,1)} %get-tuple-element.17) | data formatting | bytes 524288
  135.9 1.7 %copy.15 = f32[256,256]{1,0:T(8,128)} copy(f32[256,256]{1,0:T(8,128)} %get-tuple-element.18) | data formatting | bytes 524288
Async XLA Ops:
  88.4 45.1 %copy-start = (bf16[512,256]{1,0:T(8,128)(2,1)S(1)}, bf16[512,256]{1,0:T(8,128)(2,1)}, u32[]{:S(2)}) copy-start(bf16[512,256]{1,0:T(8,128)(2,1)} %get-tuple-element.16) | copy-start | bytes 786436

commit v2 on v1

v2 whole, which is shorter than its diff:
```python
import functools

import jax
import jax.numpy as jnp
from jax import lax
from jax.experimental import pallas as pl
from jax.experimental.pallas import tpu as pltpu
from jax.sharding import PartitionSpec as P

MESH = pl.DeviceIdType.MESH
BF = jnp.bfloat16
F32 = jnp.float32
ANY = pl.BlockSpec(memory_space=pl.ANY)
VMEM = pl.BlockSpec(memory_space=pltpu.VMEM)
SMEM = pl.BlockSpec(memory_space=pltpu.SMEM)
VMEM_BYTES = 60 * 2**20
SIDE = 128
FEAT = 256
SLOTS = 384
PAIRS_FORWARD = (SLOTS + 64) // 2
PAIRS_BACK = (SLOTS + 32) // 2
UNROLL = 8
PLACES = 512
H = (pl.ds(0, 2), pl.ds(2, 2))


class Group:
    def __init__(self, along):
        row = lax.axis_index("row")
        col = lax.axis_index("col")
        if along == "row":
            place = row
            self.device = lambda g: (g, col)
        else:
            place = lax.div(col, 2)
            core = lax.rem(col, 2)
            self.device = lambda g: (row, g * 2 + core)
            self.sibling = (row, place * 2 + 1 - core)
            self.core = core
        a = lax.div(place, 4)
        b = lax.rem(place, 4)
        up = lax.rem(b + 1, 4)
        down = lax.rem(b + 3, 4)
        far = lax.rem(b + 2, 4)
        self.own = place
        self.up, self.down, self.far = a * 4 + up, a * 4 + down, a * 4 + far
        self.other = (1 - a) * 4 + b
        self.other_up, self.other_down, self.other_far = (
            (1 - a) * 4 + up,
            (1 - a) * 4 + down,
            (1 - a) * 4 + far,
        )

    def peers(self):
        return [self.device(g) for g in (self.up, self.down, self.far, self.other)]


def greet(peers):
    barrier = pltpu.get_barrier_semaphore()
    for peer in peers:
        pl.semaphore_signal(barrier, inc=1, device_id=peer, device_id_type=MESH)
    pl.semaphore_wait(barrier, len(peers))


def ring_sum(group, send, whole, size, got, met, out, base):
    rows = lambda b: pl.ds(b * size, size)
    ring = [(group.device(g), lax.rem(g, 4)) for g in (group.up, group.down, group.far)]
    mine = lax.rem(group.own, 4)
    copies = [send(whole.at[rows(b)], got.at[k], peer) for k, (peer, b) in enumerate(ring)]
    yield
    for copy in copies:
        copy.wait_recv()
    met[0] = whole[rows(mine)] + got[0] + got[1] + got[2]
    copy = send(met.at[0], met.at[1], group.device(group.other))
    yield
    copy.wait_recv()
    spot = out.at[pl.ds(base + mine * size, size)]
    spot[...] = met[0] + met[1]
    copies = [send(spot, spot, peer) for peer, _ in ring]
    yield
    for copy in copies:
        copy.wait_recv()


def pair_then_ring_sum(group, send, whole, theirs, half, got, met, out):
    size = whole.shape[0] // 2
    mine = pl.ds(group.core * size, size)
    copy = send(whole.at[pl.ds((1 - group.core) * size, size)], theirs, group.sibling)
    yield
    copy.wait_recv()
    half[...] = whole[mine] + theirs[...]
    yield from ring_sum(group, send, half, size // 4, got, met, out, group.core * size)
    copy = send(out.at[mine], out.at[mine], group.sibling)
    yield
    copy.wait_recv()


class Sender:
    def __init__(self, send_sem, recv_sem):
        self.send_sem, self.recv_sem = send_sem, recv_sem
        self.used = 0
        self.all = []

    def __call__(self, src, dst, device):
        copy = pltpu.make_async_remote_copy(
            src_ref=src,
            dst_ref=dst,
            send_sem=self.send_sem.at[self.used],
            recv_sem=self.recv_sem.at[self.used],
            device_id=device,
            device_id_type=MESH,
        )
        self.used += 1
        self.all.append(copy)
        copy.start()
        return copy

    def finish(self):
        for copy in self.all:
            copy.wait_send()


def gather(group, send, own, spot, landed, tick=lambda: None):
    up, down, other = (group.device(g) for g in (group.up, group.down, group.other))
    here = spot(group.own)
    c_up, c_down, c_other = [None, None], [None, None], [None, None]
    for h in (0, 1):
        c_up[h] = send(own.at[H[h]], here.at[H[h]], up)
        c_down[1 - h] = send(own.at[H[1 - h]], here.at[H[1 - h]], down)
        c_other[h] = send(own.at[H[h]], here.at[H[h]], other)
    tick()
    f_up, f_down = [None, None], [None, None]
    c_up[0].wait_recv()
    far_first = send(spot(group.down).at[H[0]], spot(group.down).at[H[0]], up)
    landed(group.down, 0)
    c_down[1].wait_recv()
    far_second = send(spot(group.up).at[H[1]], spot(group.up).at[H[1]], down)
    landed(group.up, 1)
    for h in (0, 1):
        c_other[h].wait_recv()
        block = spot(group.other).at[H[h]]
        f_up[h] = send(block, block, up)
        f_down[h] = send(block, block, down)
        landed(group.other, h)
    tick()
    c_up[1].wait_recv()
    landed(group.down, 1)
    c_down[0].wait_recv()
    landed(group.up, 0)
    far_first.wait_recv()
    block = spot(group.far).at[H[0]]
    x_first = send(block, block, other)
    landed(group.far, 0)
    far_second.wait_recv()
    block = spot(group.far).at[H[1]]
    x_second = send(block, block, other)
    landed(group.far, 1)
    tick()
    for h in (0, 1):
        f_up[h].wait_recv()
        landed(group.other_down, h)
        f_down[h].wait_recv()
        landed(group.other_up, h)
    x_first.wait_recv()
    landed(group.other_far, 0)
    x_second.wait_recv()
    landed(group.other_far, 1)


def plus(target, *terms):
    total = terms[0][...].astype(F32)
    for term in terms[1:]:
        total = total + term[...].astype(F32)
    target[...] = total.astype(target.dtype)


def scatter_sum(group, send, ready, spot, got, tick=lambda: None):
    r1, r2d, r2u, r3, r4d, r4u, r5 = (got.at[k] for k in range(7))
    up, down, other = (group.device(g) for g in (group.up, group.down, group.other))
    ready(group.other_far)
    c1 = [send(spot(group.other_far).at[H[h]], r1.at[H[h]], other) for h in (0, 1)]
    ready(group.other_up)
    c2u = [send(spot(group.other_up).at[H[h]], r2d.at[H[h]], up) for h in (0, 1)]
    ready(group.other_down)
    c2d = [send(spot(group.other_down).at[H[h]], r2u.at[H[h]], down) for h in (0, 1)]
    ready(group.up)
    c4u, c4d = [None, None], [None, None]
    c4u[1] = send(spot(group.up).at[H[1]], r4d.at[H[1]], up)
    ready(group.down)
    c4d[0] = send(spot(group.down).at[H[0]], r4u.at[H[0]], down)
    ready(group.far)
    tick()
    c1[0].wait_recv()
    plus(r1.at[H[0]], r1.at[H[0]], spot(group.far).at[H[0]])
    c3u = send(r1.at[H[0]], r3.at[H[0]], up)
    tick()
    c1[1].wait_recv()
    plus(r1.at[H[1]], r1.at[H[1]], spot(group.far).at[H[1]])
    c3d = send(r1.at[H[1]], r3.at[H[1]], down)
    ready(group.other)
    tick()
    c5 = []
    for h in (0, 1):
        c2u[h].wait_recv()
        c2d[h].wait_recv()
        plus(r2d.at[H[h]], r2d.at[H[h]], r2u.at[H[h]], spot(group.other).at[H[h]])
        c5.append(send(r2d.at[H[h]], r5.at[H[h]], other))
        tick()
    c3u.wait_recv()
    plus(r3.at[H[0]], r3.at[H[0]], spot(group.up).at[H[0]])
    c4u[0] = send(r3.at[H[0]], r4d.at[H[0]], up)
    c3d.wait_recv()
    plus(r3.at[H[1]], r3.at[H[1]], spot(group.down).at[H[1]])
    c4d[1] = send(r3.at[H[1]], r4u.at[H[1]], down)
    ready(group.own)
    for copies in (c5, c4u, c4d):
        for copy in copies:
            copy.wait_recv()
    return (spot(group.own), r4d, r4u, r5)


def pair_list(key, source, live, outs, empty, pairs):
    def iota(shape, dim):
        return lax.broadcasted_iota(jnp.int32, shape, dim)

    def add(x, axis):
        return jnp.sum(x, axis=axis, keepdims=True, dtype=jnp.int32)

    def upright(x):
        n = x.shape[1]
        return add(jnp.where(iota((n, n), 0) == iota((n, n), 1), x, 0), 1)

    key_up, source_up, live_up = upright(key), upright(source), upright(live)
    square = (SLOTS, SLOTS)
    before = (key_up == key) & (iota(square, 1) < iota(square, 0))
    rank = add(jnp.where(before, live, 0), 1)
    member = jnp.where(key_up == iota((SLOTS, SIDE), 1), live_up, 0)
    held = (add(member, 0) + 1) >> 1
    tri = (SIDE, SIDE)
    start = add(jnp.where(iota(tri, 0) < iota(tri, 1), upright(held), 0), 0)
    place = jnp.where(live_up > 0, 2 * add(member * start, 1) + rank, -1)
    wide = (SLOTS, PLACES)
    hit = place == iota(wide, 1)
    slots = add(jnp.where(hit, iota(wide, 0), 0), 0)
    sources = add(jnp.where(hit, source_up - empty, 0), 0) + empty
    firsts = add(jnp.where(hit & (rank == 0), 1, 0), 0)
    last = jnp.where(held > 0, start + held - 1, pairs)
    last = jnp.concatenate([last, jnp.zeros((1, PLACES - SIDE), jnp.int32)], axis=1)
    row = iota((8, PLACES), 0)
    return jnp.where(row == 0, slots, jnp.where(row == 1, sources, jnp.where(row == 2, firsts, last)))


def tile_sums(transpose, table, tiles, panel, sums, pairs):
    block = sums.shape[1:]
    sums[pairs] = jnp.zeros(block, BF)

    def several(i, run):
        for u in range(UNROLL):
            q = i * UNROLL + u
            values = [tiles[table[0, 2 * q + k]] for k in (0, 1)]
            sources = [panel[table[1, 2 * q + k]] for k in (0, 1)]
            if transpose:
                left, right = jnp.concatenate(sources, 1), jnp.concatenate(values, 0)
            else:
                left, right = jnp.concatenate(values, 1), jnp.concatenate(sources, 0)
            run = jnp.where(table[2, 2 * q] == 1, 0.0, run)
            run = run + jnp.dot(left, right, preferred_element_type=F32)
            sums[q] = run.astype(BF)
        return run

    lax.fori_loop(0, pairs // UNROLL, several, jnp.zeros(block, F32))


def layer(
    features, weight_hbm, tiles_hbm, coords, count, cotangent_hbm,
    output_hbm, feature_hbm, weight_grad,
    tiles, panel, grads, sums_forward, sums_back, given, theirs, back, got_forward, got_back,
    lists, table_forward, table_back, weight, cotangent, output, feature_grad,
    total_hi, total_lo, own, whole, row_sum, row_got, row_met, half, half_got, col_got, col_met,
    send_sem, recv_sem, load_sem, tile_sem,
):
    rows_group, cols_group = Group("row"), Group("col")
    core, sibling = cols_group.core, cols_group.sibling
    greet(rows_group.peers() + cols_group.peers() + [sibling])
    send = Sender(send_sem, recv_sem)
    loads = [
        pltpu.make_async_copy(features, panel.at[pl.ds(rows_group.own * 4, 4)], load_sem.at[0]),
        pltpu.make_async_copy(weight_hbm, weight, load_sem.at[1]),
        pltpu.make_async_copy(cotangent_hbm, cotangent, load_sem.at[2]),
    ]
    tile_load = pltpu.make_async_copy(tiles_hbm, tiles, tile_sem)
    table_loads = [
        pltpu.make_async_copy(lists.at[0], table_forward, load_sem.at[3]),
        pltpu.make_async_copy(lists.at[1], table_back, load_sem.at[4]),
    ]

    def prepare():
        for copy in loads:
            copy.start()
        tile_load.start()
        panel[32] = jnp.zeros((SIDE, FEAT), BF)
        grads[64] = jnp.zeros((FEAT, SIDE), BF)
        tile_row, tile_col = coords[0:1], coords[1:2]
        live = jnp.where(
            lax.broadcasted_iota(jnp.int32, (1, SLOTS), 1) < count[0, 0], 1, 0
        )
        lists[0] = pair_list(tile_row, tile_col, live, 64, 32, PAIRS_FORWARD)
        lists[1] = pair_list(tile_col, tile_row, live, 32, 64, PAIRS_BACK)
        for copy in table_loads:
            copy.start()
        yield

    first = prepare()
    gather(
        rows_group, send, features, lambda g: panel.at[pl.ds(g * 4, 4)], lambda g, h: None,
        lambda: next(first, None),
    )
    for copy in loads + table_loads:
        copy.wait()
    tile_load.wait()
    tile_sums(False, table_forward, tiles, panel, sums_forward, PAIRS_FORWARD)

    group = cols_group
    order = (
        group.other_far, group.other_up, group.other_down, group.up,
        group.down, group.far, group.other, group.own,
    )
    pairs = []
    for k, g in enumerate(order):
        for t in range(4):
            given[k, t] = sums_forward[table_forward[3, (g * 2 + 1 - core) * 4 + t]]
        pairs.append(send(given.at[k], theirs.at[k], sibling))
    held = {id(g): k for k, g in enumerate(order)}

    def ready(g):
        k = held[id(g)]
        pairs[k].wait_recv()
        for t in range(4):
            mine = sums_forward[table_forward[3, (g * 2 + core) * 4 + t]]
            theirs[k, t] = (theirs[k, t].astype(F32) + mine.astype(F32)).astype(BF)

    terms = scatter_sum(group, send, ready, lambda g: theirs.at[held[id(g)]], got_forward)
    for t in range(4):
        total = terms[0][t].astype(F32)
        for term in terms[1:]:
            total = total + term[t].astype(F32)
        rows = pl.ds(t * SIDE, SIDE)
        high = total.astype(BF)
        low = (total - high.astype(F32)).astype(BF)
        total_hi[rows] = high
        total_lo[rows] = low
        hidden = jnp.dot(high, weight[...], preferred_element_type=F32) + jnp.dot(
            low, weight[...], preferred_element_type=F32
        )
        sigma = 1.0 / (1.0 + jnp.exp(-hidden))
        output[rows] = (hidden * sigma).astype(BF)
        slope = (cotangent[rows].astype(F32) * sigma * (1.0 + hidden * (1.0 - sigma))).astype(BF)
        own[rows] = slope
        grads[group.own * 8 + core * 4 + t] = lax.dot_general(
            weight[...], slope, (((1,), (1,)), ((), ())), preferred_element_type=F32
        ).astype(BF)

    def spot(g):
        return grads.at[pl.ds((g * 2 + core) * 4, 4)]

    def landed(g, h):
        block = spot(g).at[H[h]]
        shared.append(send(block, block, sibling))

    output_copy = pltpu.make_async_copy(output, output_hbm, load_sem.at[5])

    def weight_sum():
        output_copy.start()
        over = (((0,), (0,)), ((), ()))
        whole[...] = lax.dot_general(
            total_hi[...], own[...], over, preferred_element_type=F32
        ) + lax.dot_general(total_lo[...], own[...], over, preferred_element_type=F32)
        yield from ring_sum(rows_group, send, whole, FEAT // 4, row_got, row_met, row_sum, 0)

    shared = []
    stages = weight_sum()
    landed(group.own, 0)
    landed(group.own, 1)
    gather(group, send, spot(group.own), spot, landed, lambda: next(stages, None))
    for _ in stages:
        pass
    for copy in shared:
        copy.wait_recv()
    tile_sums(True, table_back, tiles, grads, sums_back, PAIRS_BACK)

    def gathered(g):
        for t in range(4):
            back[g * 4 + t] = sums_back[table_back[3, g * 4 + t]]

    stages = pair_then_ring_sum(
        cols_group, send, row_sum, half_got, half, col_got, col_met, weight_grad
    )
    terms = scatter_sum(
        rows_group, send, gathered, lambda g: back.at[pl.ds(g * 4, 4)], got_back, lambda: next(stages, None)
    )
    for t in range(4):
        total = terms[0][t].astype(F32)
        for term in terms[1:]:
            total = total + term[t].astype(F32)
        feature_grad[pl.ds(t * SIDE, SIDE)] = total.T.astype(BF)
    feature_copy = pltpu.make_async_copy(feature_grad, feature_hbm, load_sem.at[6])
    feature_copy.start()
    for _ in stages:
        pass
    send.finish()
    output_copy.wait()
    feature_copy.wait()


def local(features, weight, tiles, tile_coords, tile_counts, cotangent):
    nodes = 4 * SIDE
    blocks = lambda *lead: pltpu.VMEM(lead + (SIDE, FEAT), BF)
    turned = lambda *lead: pltpu.VMEM(lead + (FEAT, SIDE), BF)
    matrix = lambda *shape: pltpu.VMEM(shape + (FEAT,), F32)
    copies = 14 + 8 + 14 + 16 + 14 + 7 + 14 + 9
    return pl.pallas_call(
        layer,
        out_shape=(
            jax.ShapeDtypeStruct((nodes, FEAT), BF),
            jax.ShapeDtypeStruct((nodes, FEAT), BF),
            jax.ShapeDtypeStruct((FEAT, FEAT), F32),
        ),
        in_specs=[ANY, ANY, ANY, VMEM, SMEM, ANY],
        out_specs=(ANY, ANY, VMEM),
        scratch_shapes=[
            pltpu.VMEM((SLOTS, SIDE, SIDE), BF),
            blocks(33),
            turned(65),
            blocks(PAIRS_FORWARD + 1),
            turned(PAIRS_BACK + 1),
            blocks(8, 4),
            blocks(8, 4),
            turned(32),
            blocks(7, 4),
            turned(7, 4),
            pltpu.VMEM((2, 8, PLACES), jnp.int32),
            pltpu.SMEM((8, PLACES), jnp.int32),
            pltpu.SMEM((8, PLACES), jnp.int32),
            pltpu.VMEM((FEAT, FEAT), BF),
            pltpu.VMEM((nodes, FEAT), BF),
            pltpu.VMEM((nodes, FEAT), BF),
            pltpu.VMEM((nodes, FEAT), BF),
            pltpu.VMEM((nodes, FEAT), BF),
            pltpu.VMEM((nodes, FEAT), BF),
            pltpu.VMEM((nodes, FEAT), BF),
            matrix(FEAT),
            matrix(FEAT),
            matrix(3, FEAT // 4),
            matrix(2, FEAT // 4),
            matrix(FEAT // 2),
            matrix(FEAT // 2),
            matrix(3, FEAT // 8),
            matrix(2, FEAT // 8),
            pltpu.SemaphoreType.DMA((copies,)),
            pltpu.SemaphoreType.DMA((copies,)),
            pltpu.SemaphoreType.DMA((7,)),
            pltpu.SemaphoreType.DMA,
        ],
        compiler_params=pltpu.CompilerParams(
            collective_id=0, has_side_effects=True, vmem_limit_bytes=VMEM_BYTES
        ),
        name="layer",
    )(
        features.reshape(4, SIDE, FEAT), weight, tiles[0, 0], tile_coords[0, 0], tile_counts, cotangent,
    )


def solution(mesh):
    placed = (
        P(("col", "row"), None),
        P(),
        P("row", "col", None, None, None),
        P("row", "col", None, None),
        P("row", "col"),
        P(("row", "col"), None),
    )
    return jax.shard_map(
        local,
        mesh=mesh,
        in_specs=placed,
        out_specs=(P(("row", "col"), None), P(("col", "row"), None), P()),
        check_vma=False,
    )
```

time: 138 us -> 115 us (0.83)
  Pallas kernels: 132 us -> 109 us
    pallas_call x5 -> x1, Pallas kernels: 132 us -> 109 us  [local(): pl.pallas_call(layer, out_shape=(jax.ShapeDtypeStruct((nodes, FEAT), BF),...]
    unnamed x5 -> x3, local copies, waits for them, and re-layouts: 4.05 us -> 5.01 us
where the time goes in v2:
time: 115 us
  Pallas kernels  109 us (95%)
  local copies, waits for them, and re-layouts  5.01 us (4%)
  between operations  1.29 us (1%)
    pallas_call x1, Pallas kernels, local(): pl.pallas_call(layer, out_shape=(jax.ShapeDtypeStruct((nodes, FEAT), BF),...  109 us
    unnamed x3, local copies, waits for them, and re-layouts  5.01 us

profile of v2, /device:TPU:0, one launch (start us, length us, event | category | flops | bytes accessed | tf_op | source)
XLA Modules:
  0.0 115.2 jit_solution(5655435441123869455)
XLA Ops:
  1.3 108.9 %layer.1 = (bf16[512,256]{1,0:T(8,128)(2,1)}, bf16[512,256]{1,0:T(8,128)(2,1)}, f32[256,256]{1,0:T(8,128)}) custom-call(bf16[4,128,256]{2,1,0:T(8,128)(2,1)} %bitcast.4, bf16[256,256]{1,0:T(8,128)(2,1)} %weight_hbm.1, bf16[384,128,128]{2,1,0:T(8,128)(2,1)} %bitcast.3, s32[2,384]{1,0:T(2,128)} %bitcast.5, s32[1,1]{1,0:T(1,128)S(6)} %copy.12.count, ...), custom_call_target="tpu_custom_call" | custom-call | tf_op jit(solution)/shard_map/layer/pallas_call | solution.py:421
  110.2 1.7 %copy.13 = bf16[512,256]{1,0:T(8,128)(2,1)} copy(bf16[512,256]{1,0:T(8,128)(2,1)} %get-tuple-element.6) | data formatting | bytes 524288
  111.9 1.7 %copy.14 = bf16[512,256]{1,0:T(8,128)(2,1)} copy(bf16[512,256]{1,0:T(8,128)(2,1)} %get-tuple-element.7) | data formatting | bytes 524288
  113.5 1.7 %copy.15 = f32[256,256]{1,0:T(8,128)} copy(f32[256,256]{1,0:T(8,128)} %get-tuple-element.8) | data formatting | bytes 524288

commit v3 on v2

--- a/solution.py
+++ b/solution.py
@@ -19,7 +19,7 @@
 SLOTS = 384
 PAIRS_FORWARD = (SLOTS + 64) // 2
 PAIRS_BACK = (SLOTS + 32) // 2
-UNROLL = 8
+STEPS = 8
 PLACES = 512
 H = (pl.ds(0, 2), pl.ds(2, 2))
 
@@ -254,28 +254,29 @@
     block = sums.shape[1:]
     sums[pairs] = jnp.zeros(block, BF)
 
+    unroll = pairs // STEPS
+
     def several(i, run):
-        for u in range(UNROLL):
-            q = i * UNROLL + u
+        for u in range(unroll):
+            q = i * unroll + u
             values = [tiles[table[0, 2 * q + k]] for k in (0, 1)]
             sources = [panel[table[1, 2 * q + k]] for k in (0, 1)]
-            if transpose:
-                left, right = jnp.concatenate(sources, 1), jnp.concatenate(values, 0)
-            else:
-                left, right = jnp.concatenate(values, 1), jnp.concatenate(sources, 0)
+            left, right = jnp.concatenate(values, 0 if transpose else 1), jnp.concatenate(sources, 0)
             run = jnp.where(table[2, 2 * q] == 1, 0.0, run)
-            run = run + jnp.dot(left, right, preferred_element_type=F32)
+            run = run + lax.dot_general(
+                left, right, (((0 if transpose else 1,), (0,)), ((), ())), preferred_element_type=F32
+            )
             sums[q] = run.astype(BF)
         return run
 
-    lax.fori_loop(0, pairs // UNROLL, several, jnp.zeros(block, F32))
+    lax.fori_loop(0, STEPS, several, jnp.zeros(block, F32))
 
 
 def layer(
     features, weight_hbm, tiles_hbm, coords, count, cotangent_hbm,
-    output_hbm, feature_hbm, weight_grad,
+    output_hbm, feature_hbm, weight_grad_hbm,
     tiles, panel, grads, sums_forward, sums_back, given, theirs, back, got_forward, got_back,
-    lists, table_forward, table_back, weight, cotangent, output, feature_grad,
+    lists, table_forward, table_back, weight, cotangent, output, feature_grad, weight_grad,
     total_hi, total_lo, own, whole, row_sum, row_got, row_met, half, half_got, col_got, col_met,
     send_sem, recv_sem, load_sem, tile_sem,
 ):
@@ -299,7 +300,7 @@
             copy.start()
         tile_load.start()
         panel[32] = jnp.zeros((SIDE, FEAT), BF)
-        grads[64] = jnp.zeros((FEAT, SIDE), BF)
+        grads[64] = jnp.zeros((SIDE, FEAT), BF)
         tile_row, tile_col = coords[0:1], coords[1:2]
         live = jnp.where(
             lax.broadcasted_iota(jnp.int32, (1, SLOTS), 1) < count[0, 0], 1, 0
@@ -357,7 +358,7 @@
         slope = (cotangent[rows].astype(F32) * sigma * (1.0 + hidden * (1.0 - sigma))).astype(BF)
         own[rows] = slope
         grads[group.own * 8 + core * 4 + t] = lax.dot_general(
-            weight[...], slope, (((1,), (1,)), ((), ())), preferred_element_type=F32
+            slope, weight[...], (((1,), (1,)), ((), ())), preferred_element_type=F32
         ).astype(BF)
 
     def spot(g):
@@ -402,42 +403,51 @@
         total = terms[0][t].astype(F32)
         for term in terms[1:]:
             total = total + term[t].astype(F32)
-        feature_grad[pl.ds(t * SIDE, SIDE)] = total.T.astype(BF)
+        feature_grad[pl.ds(t * SIDE, SIDE)] = total.astype(BF)
     feature_copy = pltpu.make_async_copy(feature_grad, feature_hbm, load_sem.at[6])
     feature_copy.start()
     for _ in stages:
         pass
+    weight_copy = pltpu.make_async_copy(weight_grad, weight_grad_hbm, load_sem.at[7])
+    weight_copy.start()
     send.finish()
     output_copy.wait()
     feature_copy.wait()
+    weight_copy.wait()
+
+
+def deliver(*refs):
+    count = len(refs) // 2
+    for k in range(count):
+        refs[count + k][...] = refs[k][...]
 
 
 def local(features, weight, tiles, tile_coords, tile_counts, cotangent):
     nodes = 4 * SIDE
     blocks = lambda *lead: pltpu.VMEM(lead + (SIDE, FEAT), BF)
-    turned = lambda *lead: pltpu.VMEM(lead + (FEAT, SIDE), BF)
     matrix = lambda *shape: pltpu.VMEM(shape + (FEAT,), F32)
     copies = 14 + 8 + 14 + 16 + 14 + 7 + 14 + 9
-    return pl.pallas_call(
+    shapes = (
+        jax.ShapeDtypeStruct((nodes, FEAT), BF),
+        jax.ShapeDtypeStruct((nodes, FEAT), BF),
+        jax.ShapeDtypeStruct((FEAT, FEAT), F32),
+    )
+    results = pl.pallas_call(
         layer,
-        out_shape=(
-            jax.ShapeDtypeStruct((nodes, FEAT), BF),
-            jax.ShapeDtypeStruct((nodes, FEAT), BF),
-            jax.ShapeDtypeStruct((FEAT, FEAT), F32),
-        ),
+        out_shape=shapes,
         in_specs=[ANY, ANY, ANY, VMEM, SMEM, ANY],
-        out_specs=(ANY, ANY, VMEM),
+        out_specs=(ANY, ANY, ANY),
         scratch_shapes=[
             pltpu.VMEM((SLOTS, SIDE, SIDE), BF),
             blocks(33),
-            turned(65),
+            blocks(65),
             blocks(PAIRS_FORWARD + 1),
-            turned(PAIRS_BACK + 1),
+            blocks(PAIRS_BACK + 1),
             blocks(8, 4),
             blocks(8, 4),
-            turned(32),
+            blocks(32),
             blocks(7, 4),
-            turned(7, 4),
+            blocks(7, 4),
             pltpu.VMEM((2, 8, PLACES), jnp.int32),
             pltpu.SMEM((8, PLACES), jnp.int32),
             pltpu.SMEM((8, PLACES), jnp.int32),
@@ -445,6 +455,7 @@
             pltpu.VMEM((nodes, FEAT), BF),
             pltpu.VMEM((nodes, FEAT), BF),
             pltpu.VMEM((nodes, FEAT), BF),
+            matrix(FEAT),
             pltpu.VMEM((nodes, FEAT), BF),
             pltpu.VMEM((nodes, FEAT), BF),
             pltpu.VMEM((nodes, FEAT), BF),
@@ -458,7 +469,7 @@
             matrix(2, FEAT // 8),
             pltpu.SemaphoreType.DMA((copies,)),
             pltpu.SemaphoreType.DMA((copies,)),
-            pltpu.SemaphoreType.DMA((7,)),
+            pltpu.SemaphoreType.DMA((8,)),
             pltpu.SemaphoreType.DMA,
         ],
         compiler_params=pltpu.CompilerParams(
@@ -468,6 +479,13 @@
     )(
         features.reshape(4, SIDE, FEAT), weight, tiles[0, 0], tile_coords[0, 0], tile_counts, cotangent,
     )
+    return pl.pallas_call(
+        deliver,
+        out_shape=shapes,
+        in_specs=[VMEM, VMEM, VMEM],
+        out_specs=(VMEM, VMEM, VMEM),
+        name="deliver",
+    )(*results)
 
 
 def solution(mesh):

time: 115 us -> 103 us (0.90)
  Pallas kernels: 109 us -> 101 us
  local copies, waits for them, and re-layouts: 5.01 us -> 0 us
    pallas_call x1 -> x2, Pallas kernels: 109 us -> 101 us  [the longest x1 99.2 us: local(): pl.pallas_call(layer, out_shape=shapes, in_specs=[ANY, ANY, ANY, VMEM, SM...]
    unnamed x3 -> x0, local copies, waits for them, and re-layouts: 5.01 us -> none
where the time goes in v3:
time: 103 us; the launch traced here: 102 us
  Pallas kernels  101 us (98%)
  between operations  1.29 us (1%)
    pallas_call x1, Pallas kernels, local(): pl.pallas_call(layer, out_shape=shapes, in_specs=[ANY, ANY, ANY, VMEM, SM...  99.2 us

profile of v3, /device:TPU:0, one launch (start us, length us, event | category | flops | bytes accessed | tf_op | source)
XLA Modules:
  0.0 102.5 jit_solution(14744357803556013967)
XLA Ops:
  1.3 99.2 %layer.1 = (bf16[512,256]{1,0:T(8,128)(2,1)}, bf16[512,256]{1,0:T(8,128)(2,1)}, f32[256,256]{1,0:T(8,128)}) custom-call(bf16[4,128,256]{2,1,0:T(8,128)(2,1)} %bitcast.4, bf16[256,256]{1,0:T(8,128)(2,1)} %weight_hbm.1, bf16[384,128,128]{2,1,0:T(8,128)(2,1)} %bitcast.3, s32[2,384]{1,0:T(2,128)} %bitcast.5, s32[1,1]{1,0:T(1,128)S(6)} %copy.9.count, ...), custom_call_target="tpu_custom_call" | custom-call | tf_op jit(solution)/shard_map/layer/pallas_call | solution.py:435
  100.5 2.0 %deliver.1 = (bf16[512,256]{1,0:T(8,128)(2,1)}, bf16[512,256]{1,0:T(8,128)(2,1)}, f32[256,256]{1,0:T(8,128)}) custom-call(bf16[512,256]{1,0:T(8,128)(2,1)} %get-tuple-element.6.refs_0_, bf16[512,256]{1,0:T(8,128)(2,1)} %get-tuple-element.7.refs_1_, f32[256,256]{1,0:T(8,128)} %get-tuple-element.8.refs_2_), custom_call_target="tpu_custom_call" | custom-call | tf_op jit(solution)/shard_map/deliver/pallas_call | solution.py:482

commit v4 on v3

--- a/solution.py
+++ b/solution.py
@@ -19,7 +19,8 @@
 SLOTS = 384
 PAIRS_FORWARD = (SLOTS + 64) // 2
 PAIRS_BACK = (SLOTS + 32) // 2
-STEPS = 8
+CUTS = (0, 66, 132, 198, PAIRS_FORWARD)
+STEPS = 2
 PLACES = 512
 H = (pl.ds(0, 2), pl.ds(2, 2))
 
@@ -93,6 +94,16 @@
     copy = send(out.at[mine], out.at[mine], group.sibling)
     yield
     copy.wait_recv()
+
+
+def in_turn(tile_row):
+    col = lax.axis_index("col")
+    core, b, a = lax.rem(col, 2), lax.rem(lax.div(col, 2), 4), lax.div(col, 8)
+    side = jnp.where((tile_row >> 5) == a, 4, 0)
+    kin = jnp.where(((tile_row >> 2) & 1) == core, 8, 0)
+    steps = (((tile_row >> 3) & 3) + 4 - b) & 3
+    place = jnp.where(steps == 0, 3, jnp.where(steps == 1, 0, jnp.where(steps == 2, 2, 1)))
+    return (kin + side + place) * 4 + (tile_row & 3)
 
 
 class Sender:
@@ -177,12 +188,12 @@
 def scatter_sum(group, send, ready, spot, got, tick=lambda: None):
     r1, r2d, r2u, r3, r4d, r4u, r5 = (got.at[k] for k in range(7))
     up, down, other = (group.device(g) for g in (group.up, group.down, group.other))
-    ready(group.other_far)
-    c1 = [send(spot(group.other_far).at[H[h]], r1.at[H[h]], other) for h in (0, 1)]
     ready(group.other_up)
     c2u = [send(spot(group.other_up).at[H[h]], r2d.at[H[h]], up) for h in (0, 1)]
     ready(group.other_down)
     c2d = [send(spot(group.other_down).at[H[h]], r2u.at[H[h]], down) for h in (0, 1)]
+    ready(group.other_far)
+    c1 = [send(spot(group.other_far).at[H[h]], r1.at[H[h]], other) for h in (0, 1)]
     ready(group.up)
     c4u, c4d = [None, None], [None, None]
     c4u[1] = send(spot(group.up).at[H[1]], r4d.at[H[1]], up)
@@ -250,26 +261,27 @@
     return jnp.where(row == 0, slots, jnp.where(row == 1, sources, jnp.where(row == 2, firsts, last)))
 
 
-def tile_sums(transpose, table, tiles, panel, sums, pairs):
-    block = sums.shape[1:]
-    sums[pairs] = jnp.zeros(block, BF)
-
-    unroll = pairs // STEPS
+def tile_step(transpose, table, tiles, panel, sums, q, run):
+    values = [tiles[table[0, 2 * q + k]] for k in (0, 1)]
+    sources = [panel[table[1, 2 * q + k]] for k in (0, 1)]
+    left, right = jnp.concatenate(values, 0 if transpose else 1), jnp.concatenate(sources, 0)
+    run = jnp.where(table[2, 2 * q] == 1, 0.0, run)
+    run = run + lax.dot_general(
+        left, right, (((0 if transpose else 1,), (0,)), ((), ())), preferred_element_type=F32
+    )
+    sums[q] = run.astype(BF)
+    return run
+
+
+def tile_sums(transpose, table, tiles, panel, sums, first, last, run, steps):
+    unroll = (last - first) // steps
 
     def several(i, run):
         for u in range(unroll):
-            q = i * unroll + u
-            values = [tiles[table[0, 2 * q + k]] for k in (0, 1)]
-            sources = [panel[table[1, 2 * q + k]] for k in (0, 1)]
-            left, right = jnp.concatenate(values, 0 if transpose else 1), jnp.concatenate(sources, 0)
-            run = jnp.where(table[2, 2 * q] == 1, 0.0, run)
-            run = run + lax.dot_general(
-                left, right, (((0 if transpose else 1,), (0,)), ((), ())), preferred_element_type=F32
-            )
-            sums[q] = run.astype(BF)
+            run = tile_step(transpose, table, tiles, panel, sums, first + i * unroll + u, run)
         return run
 
-    lax.fori_loop(0, STEPS, several, jnp.zeros(block, F32))
+    return lax.fori_loop(0, steps, several, run)
 
 
 def layer(
@@ -305,7 +317,7 @@
         live = jnp.where(
             lax.broadcasted_iota(jnp.int32, (1, SLOTS), 1) < count[0, 0], 1, 0
         )
-        lists[0] = pair_list(tile_row, tile_col, live, 64, 32, PAIRS_FORWARD)
+        lists[0] = pair_list(in_turn(tile_row), tile_col, live, 64, 32, PAIRS_FORWARD)
         lists[1] = pair_list(tile_col, tile_row, live, 32, 64, PAIRS_BACK)
         for copy in table_loads:
             copy.start()
@@ -319,25 +331,36 @@
     for copy in loads + table_loads:
         copy.wait()
     tile_load.wait()
-    tile_sums(False, table_forward, tiles, panel, sums_forward, PAIRS_FORWARD)
-
     group = cols_group
     order = (
-        group.other_far, group.other_up, group.other_down, group.up,
-        group.down, group.far, group.other, group.own,
-    )
+        group.other_up, group.other_down, group.other_far, group.other,
+        group.up, group.down, group.far, group.own,
+    )
+    held = {id(g): k for k, g in enumerate(order)}
     pairs = []
-    for k, g in enumerate(order):
+
+    def give(k):
         for t in range(4):
-            given[k, t] = sums_forward[table_forward[3, (g * 2 + 1 - core) * 4 + t]]
+            given[k, t] = sums_forward[table_forward[3, k * 4 + t]]
         pairs.append(send(given.at[k], theirs.at[k], sibling))
-    held = {id(g): k for k, g in enumerate(order)}
+
+    block = (SIDE, FEAT)
+    sums_forward[PAIRS_FORWARD] = jnp.zeros(block, BF)
+    run = jnp.zeros(block, F32)
+    for k, (begin, end) in enumerate(zip(CUTS[:-1], CUTS[1:])):
+        run = tile_sums(
+            False, table_forward, tiles, panel, sums_forward, begin, end, run, 2
+        )
+        if k < 3:
+            give(k)
+    for k in range(3, 8):
+        give(k)
 
     def ready(g):
         k = held[id(g)]
         pairs[k].wait_recv()
         for t in range(4):
-            mine = sums_forward[table_forward[3, (g * 2 + core) * 4 + t]]
+            mine = sums_forward[table_forward[3, (k + 8) * 4 + t]]
             theirs[k, t] = (theirs[k, t].astype(F32) + mine.astype(F32)).astype(BF)
 
     terms = scatter_sum(group, send, ready, lambda g: theirs.at[held[id(g)]], got_forward)
@@ -387,7 +410,10 @@
         pass
     for copy in shared:
         copy.wait_recv()
-    tile_sums(True, table_back, tiles, grads, sums_back, PAIRS_BACK)
+    sums_back[PAIRS_BACK] = jnp.zeros(block, BF)
+    tile_sums(
+        True, table_back, tiles, grads, sums_back, 0, PAIRS_BACK, jnp.zeros(block, F32), STEPS
+    )
 
     def gathered(g):
         for t in range(4):
@@ -417,9 +443,18 @@
 
 
 def deliver(*refs):
-    count = len(refs) // 2
+    count = (len(refs) - 2) // 3
+    into, out = refs[-2], refs[-1]
+    sources, targets, held = refs[:count], refs[count : 2 * count], refs[2 * count : 3 * count]
+    first = [pltpu.make_async_copy(sources[k], held[k], into.at[k]) for k in range(count)]
+    second = [pltpu.make_async_copy(held[k], targets[k], out.at[k]) for k in range(count)]
+    for copy in first:
+        copy.start()
     for k in range(count):
-        refs[count + k][...] = refs[k][...]
+        first[k].wait()
+        second[k].start()
+    for copy in second:
+        copy.wait()
 
 
 def local(features, weight, tiles, tile_coords, tile_counts, cotangent):
@@ -482,8 +517,10 @@
     return pl.pallas_call(
         deliver,
         out_shape=shapes,
-        in_specs=[VMEM, VMEM, VMEM],
-        out_specs=(VMEM, VMEM, VMEM),
+        in_specs=[ANY, ANY, ANY],
+        out_specs=(ANY, ANY, ANY),
+        scratch_shapes=[pltpu.VMEM(shape.shape, shape.dtype) for shape in shapes]
+        + [pltpu.SemaphoreType.DMA((3,)), pltpu.SemaphoreType.DMA((3,))],
         name="deliver",
     )(*results)
 

time: 103 us -> 98.4 us (0.955)
  Pallas kernels: 101 us -> 96.9 us
    pallas_call x1, Pallas kernels: 99.2 us -> 95 us  [local(): pl.pallas_call(layer, out_shape=shapes, in_specs=[ANY, ANY, ANY, VMEM, SM...]
where the time goes in v4:
time: 98.4 us; the launch traced here: 98.2 us
  Pallas kernels  96.9 us (98%)
  between operations  1.29 us (1%)
    pallas_call x1, Pallas kernels, local(): pl.pallas_call(layer, out_shape=shapes, in_specs=[ANY, ANY, ANY, VMEM, SM...  95 us

profile of v4, /device:TPU:0, one launch (start us, length us, event | category | flops | bytes accessed | tf_op | source)
XLA Modules:
  0.0 98.2 jit_solution(14033626771162717297)
XLA Ops:
  1.3 95.0 %layer.1 = (bf16[512,256]{1,0:T(8,128)(2,1)}, bf16[512,256]{1,0:T(8,128)(2,1)}, f32[256,256]{1,0:T(8,128)}) custom-call(bf16[4,128,256]{2,1,0:T(8,128)(2,1)} %bitcast.4, bf16[256,256]{1,0:T(8,128)(2,1)} %weight_hbm.1, bf16[384,128,128]{2,1,0:T(8,128)(2,1)} %bitcast.3, s32[2,384]{1,0:T(2,128)} %bitcast.5, s32[1,1]{1,0:T(1,128)S(6)} %copy.9.count, ...), custom_call_target="tpu_custom_call" | custom-call | tf_op jit(solution)/shard_map/layer/pallas_call | solution.py:470
  96.3 1.9 %deliver.1 = (bf16[512,256]{1,0:T(8,128)(2,1)}, bf16[512,256]{1,0:T(8,128)(2,1)}, f32[256,256]{1,0:T(8,128)}) custom-call(bf16[512,256]{1,0:T(8,128)(2,1)} %get-tuple-element.6.refs_0_, bf16[512,256]{1,0:T(8,128)(2,1)} %get-tuple-element.7.refs_1_, f32[256,256]{1,0:T(8,128)} %get-tuple-element.8.refs_2_), custom_call_target="tpu_custom_call" | custom-call | tf_op jit(solution)/shard_map/deliver/pallas_call | solution.py:517

commit v5 on v4

--- a/solution.py
+++ b/solution.py
@@ -131,14 +131,18 @@
             copy.wait_send()
 
 
-def gather(group, send, own, spot, landed, tick=lambda: None):
+def gather(group, send, own, spot, landed, tick=lambda: None, make=lambda h: None):
     up, down, other = (group.device(g) for g in (group.up, group.down, group.other))
     here = spot(group.own)
     c_up, c_down, c_other = [None, None], [None, None], [None, None]
-    for h in (0, 1):
-        c_up[h] = send(own.at[H[h]], here.at[H[h]], up)
-        c_down[1 - h] = send(own.at[H[1 - h]], here.at[H[1 - h]], down)
-        c_other[h] = send(own.at[H[h]], here.at[H[h]], other)
+    make(0)
+    c_up[0] = send(own.at[H[0]], here.at[H[0]], up)
+    c_other[0] = send(own.at[H[0]], here.at[H[0]], other)
+    make(1)
+    c_down[1] = send(own.at[H[1]], here.at[H[1]], down)
+    c_up[1] = send(own.at[H[1]], here.at[H[1]], up)
+    c_down[0] = send(own.at[H[0]], here.at[H[0]], down)
+    c_other[1] = send(own.at[H[1]], here.at[H[1]], other)
     tick()
     f_up, f_down = [None, None], [None, None]
     c_up[0].wait_recv()
@@ -364,25 +368,27 @@
             theirs[k, t] = (theirs[k, t].astype(F32) + mine.astype(F32)).astype(BF)
 
     terms = scatter_sum(group, send, ready, lambda g: theirs.at[held[id(g)]], got_forward)
-    for t in range(4):
-        total = terms[0][t].astype(F32)
-        for term in terms[1:]:
-            total = total + term[t].astype(F32)
-        rows = pl.ds(t * SIDE, SIDE)
-        high = total.astype(BF)
-        low = (total - high.astype(F32)).astype(BF)
-        total_hi[rows] = high
-        total_lo[rows] = low
-        hidden = jnp.dot(high, weight[...], preferred_element_type=F32) + jnp.dot(
-            low, weight[...], preferred_element_type=F32
-        )
-        sigma = 1.0 / (1.0 + jnp.exp(-hidden))
-        output[rows] = (hidden * sigma).astype(BF)
-        slope = (cotangent[rows].astype(F32) * sigma * (1.0 + hidden * (1.0 - sigma))).astype(BF)
-        own[rows] = slope
-        grads[group.own * 8 + core * 4 + t] = lax.dot_general(
-            slope, weight[...], (((1,), (1,)), ((), ())), preferred_element_type=F32
-        ).astype(BF)
+    def make(h):
+        for t in (2 * h, 2 * h + 1):
+            total = terms[0][t].astype(F32)
+            for term in terms[1:]:
+                total = total + term[t].astype(F32)
+            rows = pl.ds(t * SIDE, SIDE)
+            high = total.astype(BF)
+            low = (total - high.astype(F32)).astype(BF)
+            total_hi[rows] = high
+            total_lo[rows] = low
+            hidden = jnp.dot(high, weight[...], preferred_element_type=F32) + jnp.dot(
+                low, weight[...], preferred_element_type=F32
+            )
+            sigma = 1.0 / (1.0 + jnp.exp(-hidden))
+            output[rows] = (hidden * sigma).astype(BF)
+            slope = (cotangent[rows].astype(F32) * sigma * (1.0 + hidden * (1.0 - sigma))).astype(BF)
+            own[rows] = slope
+            grads[group.own * 8 + core * 4 + t] = lax.dot_general(
+                slope, weight[...], (((1,), (1,)), ((), ())), preferred_element_type=F32
+            ).astype(BF)
+        landed(group.own, h)
 
     def spot(g):
         return grads.at[pl.ds((g * 2 + core) * 4, 4)]
@@ -403,9 +409,7 @@
 
     shared = []
     stages = weight_sum()
-    landed(group.own, 0)
-    landed(group.own, 1)
-    gather(group, send, spot(group.own), spot, landed, lambda: next(stages, None))
+    gather(group, send, spot(group.own), spot, landed, lambda: next(stages, None), make)
     for _ in stages:
         pass
     for copy in shared:

time: 98.4 us -> 98.2 us (level)
  no operation moved by 1% of the time
where the time goes in v5:
time: 98.2 us; the launch traced here: 98 us
  Pallas kernels  96.7 us (98%)
  between operations  1.29 us (1%)
    pallas_call x1, Pallas kernels, local(): pl.pallas_call(layer, out_shape=shapes, in_specs=[ANY, ANY, ANY, VMEM, SM...  94.9 us

profile of v5, /device:TPU:0, one launch (start us, length us, event | category | flops | bytes accessed | tf_op | source)
XLA Modules:
  0.0 98.0 jit_solution(3075553147092524446)
XLA Ops:
  1.3 94.9 %layer.1 = (bf16[512,256]{1,0:T(8,128)(2,1)}, bf16[512,256]{1,0:T(8,128)(2,1)}, f32[256,256]{1,0:T(8,128)}) custom-call(bf16[4,128,256]{2,1,0:T(8,128)(2,1)} %bitcast.4, bf16[256,256]{1,0:T(8,128)(2,1)} %weight_hbm.1, bf16[384,128,128]{2,1,0:T(8,128)(2,1)} %bitcast.3, s32[2,384]{1,0:T(2,128)} %bitcast.5, s32[1,1]{1,0:T(1,128)S(6)} %copy.9.count, ...), custom_call_target="tpu_custom_call" | custom-call | tf_op jit(solution)/shard_map/layer/pallas_call | solution.py:474
  96.1 1.9 %deliver.1 = (bf16[512,256]{1,0:T(8,128)(2,1)}, bf16[512,256]{1,0:T(8,128)(2,1)}, f32[256,256]{1,0:T(8,128)}) custom-call(bf16[512,256]{1,0:T(8,128)(2,1)} %get-tuple-element.6.refs_0_, bf16[512,256]{1,0:T(8,128)(2,1)} %get-tuple-element.7.refs_1_, f32[256,256]{1,0:T(8,128)} %get-tuple-element.8.refs_2_), custom_call_target="tpu_custom_call" | custom-call | tf_op jit(solution)/shard_map/deliver/pallas_call | solution.py:521
